TPU v7x, 32 devices: a whole 2x2x4 slice. The times are simulated.
32 devices in a mesh: sub: 8 (over z, y), mem: 4 (over x, core).
Axes of the slice: x: 2, y: 2, z: 4, core: 2. Of those that a mesh axis runs over, the one named last changes fastest.
Arguments:
- static_control: float32 [4, 4, 64, 1536], P('mem', None, 'sub'), may hold values from -6 to 6
- alpha_field: float32 [4, 4, 64, 1536], P('mem', None, 'sub'), may hold values from -6 to 6
- perturbations: bfloat16 [4, 4, 4, 64, 1536], P('mem', None, None, 'sub'), may hold values from -6 to 6
- static_scale: float32 [4, 4], P('mem'), may hold values from 0.5 to 2
- length_x: float32 [4], replicated, may hold values from 0.5 to 1
- length_y: float32 [4], replicated, may hold values from 2 to 16
- lengths: int32 [8], replicated, may hold values from 1 to 8, 48 in all
Outputs:
- increment: float32 [4, 4, 64, 1536], P('mem', None, 'sub')
Inputs may be any that keep to these rules, and one draw needn't show every extreme that they name: lengths[d] is the number of grid rows of subdomain d; they sum to 48 and the largest is exactly 8.
All inputs are finite; a program needn't handle non-finite values.
Results may differ from a plain program's by a relative error of at most 0.0003.
Values sent between devices are 32-bit elements; how exact they have to be, the bound alone decides.
A program may use at most 64 MiB of HBM per device.

v0:
```python
import math

import jax
import jax.numpy as jnp
from jax import lax
from jax.sharding import PartitionSpec as P

ROWS_DEV = 6


def recurse(values, length_scale, reverse):
    full_shape = values.shape
    line_len = full_shape[-1]
    block_len = 128 if line_len % 128 == 0 else line_len
    block_count = line_len // block_len
    if reverse:
        values = jnp.flip(values, -1)
    offsets = jnp.arange(block_len, dtype=jnp.float32)
    lagged = offsets[:, None] - offsets[None, :]
    inverse = 1.0 / length_scale
    decays = jnp.exp(-inverse)
    kernel = jnp.where(
        lagged[None] >= 0.0,
        (1.0 - decays)[:, None, None]
        * jnp.exp(-jnp.maximum(lagged, 0.0)[None] * inverse[:, None, None]),
        0.0,
    )
    carry_w = jnp.exp(-(offsets[None, :] + 1.0) * inverse[:, None])
    powers = [kernel]
    for power_idx in range(3):
        powers.append(
            jnp.einsum("lij,ljk->lik", powers[-1], kernel, precision=lax.Precision.HIGHEST)
        )
    carried = [carry_w]
    for power_idx in range(3):
        carried.append(
            jnp.einsum("lij,lj->li", kernel, carried[-1], precision=lax.Precision.HIGHEST)
        )
    last_rows = jnp.stack([powers[0][:, -1, :], powers[1][:, -1, :], powers[2][:, -1, :]], 1)
    full_power = powers[3]
    blocks = jnp.moveaxis(values.reshape(full_shape[:-1] + (block_count, block_len)), -2, 0)

    def advance(states, current):
        lasts = jnp.einsum("blrj,lkj->blrk", current, last_rows, precision=lax.Precision.HIGHEST)
        output = jnp.einsum("blrj,lij->blri", current, full_power, precision=lax.Precision.HIGHEST)
        for section_idx in range(4):
            output = (
                output + states[section_idx][..., None] * carried[3 - section_idx][None, :, None, :]
            )
        finals = []
        for section_idx in range(3):
            entry = lasts[..., section_idx]
            for source_idx in range(section_idx + 1):
                entry = (
                    entry
                    + states[source_idx] * carried[section_idx - source_idx][None, :, None, -1]
                )
            finals.append(entry)
        finals.append(output[..., -1])
        return (tuple(finals), output)

    zero_state = tuple((jnp.zeros(full_shape[:-1], jnp.float32) for section_idx in range(4)))
    unused, filtered = lax.scan(advance, zero_state, blocks)
    filtered = jnp.moveaxis(filtered, 0, -2).reshape(full_shape)
    if reverse:
        filtered = jnp.flip(filtered, -1)
    return filtered


def smooth(values, length_scale):
    return recurse(recurse(values, length_scale, False), length_scale, True)


def row_index(lengths, rows_max, row_total):
    starts = jnp.cumsum(lengths) - lengths
    compact = jnp.arange(row_total, dtype=jnp.int32)
    owners = jnp.sum((starts[None, :] <= compact[:, None]).astype(jnp.int32), axis=1) - 1
    chosen = (owners[:, None] == jnp.arange(lengths.shape[0], dtype=jnp.int32)[None, :]).astype(
        jnp.int32
    )
    first_row = jnp.sum(chosen * starts[None, :], axis=1)
    return owners * rows_max + compact - first_row


def body(static_control, alpha_field, perturbations, static_scale, length_x, length_y, lengths):
    rows_max = static_control.shape[2]
    sub_count = lax.axis_size("sub")
    positions = row_index(lengths, rows_max, ROWS_DEV * sub_count)
    here = lax.axis_index("sub")
    own_rows = jnp.sum(jnp.where(jnp.arange(sub_count, dtype=jnp.int32) == here, lengths, 0))
    row_valid = (jnp.arange(rows_max, dtype=jnp.int32) < own_rows).astype(jnp.float32)[
        None, None, :, None
    ]
    factor = jnp.sqrt(length_x * length_y)[None, :, None, None]

    def column_filter(pencils):
        gathered = jnp.take(pencils, positions, axis=2)
        along_y = jnp.moveaxis(smooth(jnp.moveaxis(gathered, 2, 3), length_y), 3, 2)
        return jnp.zeros(pencils.shape, jnp.float32).at[:, :, positions, :].set(along_y * factor)

    vars_here = static_control.shape[0]
    static_x = smooth(static_control * row_valid, length_x)
    static_done = lax.all_to_all(
        column_filter(lax.all_to_all(static_x, "sub", split_axis=3, concat_axis=2, tiled=True)),
        "sub",
        split_axis=2,
        concat_axis=3,
        tiled=True,
    )
    member_x = smooth(alpha_field * row_valid, length_x)
    member_done = lax.all_to_all(
        column_filter(lax.all_to_all(member_x, "sub", split_axis=3, concat_axis=2, tiled=True)),
        "sub",
        split_axis=2,
        concat_axis=3,
        tiled=True,
    )
    partial_sum = perturbations[0].astype(jnp.float32) * member_done[0][None]
    member_count = alpha_field.shape[0] * lax.axis_size("mem")
    summed = lax.psum(partial_sum, "mem")
    own_sum = lax.dynamic_slice_in_dim(summed, lax.axis_index("mem") * vars_here, vars_here, 0)
    return static_scale[:, :, None, None] * static_done + own_sum * (1.0 / math.sqrt(member_count))


def solution(mesh):
    return jax.shard_map(
        body,
        mesh=mesh,
        in_specs=(
            P("mem", None, "sub", None),
            P("mem", None, "sub", None),
            P("mem", None, None, "sub", None),
            P("mem", None),
            P(),
            P(),
            P(),
        ),
        out_specs=P("mem", None, "sub", None),
        check_vma=False,
    )
```

profile of v0, /device:TPU:0, one launch (start us, length us, event | category | flops | bytes accessed | tf_op | source)
XLA Modules:
  0.0 193.3 jit_solution(12618842496542741733)
XLA Ops:
  6.6 1.4 exponential_subtract_fusion
  12.1 1.3 fusion.154
  14.3 14.7 %while.14 = (s32[]{:T(128)}, f32[1,4,8]{2,1,0:T(4,128)S(1)}, f32[1,4,8]{2,1,0:T(4,128)S(1)}, f32[1,4,8]{2,1,0:T(4,128)S(1)}, f32[1,4,8]{2,1,0:T(4,128)S(1)}, /*i...) while((s32[]{:T(128)}, f32[1,4,8]{2,1,0:T(4,128)S(1)}, ...), condition=%wide.region_10.12_spmd.clone, body=%wide.region_9.11_spmd.clone.sunk | while | flops 6472163 | bytes 368811 | solution.py:63
  28.9 0.9 rev.25
  29.9 14.7 %while.15 = (s32[]{:T(128)}, f32[1,4,8]{2,1,0:T(4,128)S(1)}, f32[1,4,8]{2,1,0:T(4,128)S(1)}, f32[1,4,8]{2,1,0:T(4,128)S(1)}, f32[1,4,8]{2,1,0:T(4,128)S(1)}, /*i...) while((s32[]{:T(128)}, f32[1,4,8]{2,1,0:T(4,128)S(1)}, ...), condition=%wide.region_12.14_spmd.clone, body=%wide.region_11.13_spmd.clone.sunk | while | flops 6472163 | bytes 368811 | solution.py:63
  44.5 0.9 rev.26
  45.4 2.7 %copy.169 = f32[1,4,8,1536]{2,1,0,3:T(4,128)} copy(f32[1,4,8,1536]{3,2,1,0:T(8,128)S(1)} %rev.26) | data formatting | bytes 393216 | tf_op jit(solution)/shard_map/jit(_flip)/rev | solution.py:66
  48.1 5.7 %reshape.592 = f32[8,1,6144]{2,1,0:T(1,128)} reshape(f32[1536,1,4,8]{3,2,1,0:T(4,128)} %bitcast.579) | data formatting | bytes 393216
  53.8 7.3 %all-to-all-start.2 = ((f32[8,1,6144]{2,1,0:T(1,128)}), f32[8,1,6144]{2,1,0:T(1,128)S(1)}, u32[]{:S(2)}, u32[]{:S(2)}) async-start(f32[8,1,6144]{2,1,0:T(1,128)} %reshape.592), calls=%async_computation.2 | async-start | bytes 393216 | tf_op jit(solution)/shard_map/all_to_all | solution.py:112
  63.1 14.7 %while.12 = (s32[]{:T(128)}, f32[1,4,8]{2,1,0:T(4,128)S(1)}, f32[1,4,8]{2,1,0:T(4,128)S(1)}, f32[1,4,8]{2,1,0:T(4,128)S(1)}, f32[1,4,8]{2,1,0:T(4,128)S(1)}, /*i...) while((s32[]{:T(128)}, f32[1,4,8]{2,1,0:T(4,128)S(1)}, ...), condition=%wide.region_5.6_spmd.clone, body=%wide.region_4.5_spmd.clone.sunk | while | flops 6472163 | bytes 368811 | solution.py:63
  77.7 0.9 rev.22
  78.7 14.7 %while.13 = (s32[]{:T(128)}, f32[1,4,8]{2,1,0:T(4,128)S(1)}, f32[1,4,8]{2,1,0:T(4,128)S(1)}, f32[1,4,8]{2,1,0:T(4,128)S(1)}, f32[1,4,8]{2,1,0:T(4,128)S(1)}, /*i...) while((s32[]{:T(128)}, f32[1,4,8]{2,1,0:T(4,128)S(1)}, ...), condition=%wide.region_7.8_spmd.clone, body=%wide.region_6.7_spmd.clone.sunk | while | flops 6472163 | bytes 368811 | solution.py:63
  94.2 1.2 copy.157
  95.5 4.3 %reshape.594 = f32[8,1,6144]{2,1,0:T(1,128)} reshape(f32[1536,1,4,8]{3,2,1,0:T(4,128)S(1)} %bitcast.580) | data formatting | bytes 393216
  103.1 0.9 fusion.118
  104.0 6.0 %all-to-all-start = ((f32[8,1,6144]{2,1,0:T(1,128)}), f32[8,1,6144]{2,1,0:T(1,128)}, u32[]{:S(2)}, u32[]{:S(2)}) async-start(f32[8,1,6144]{2,1,0:T(1,128)} %reshape.594), calls=%async_computation | async-start | bytes 393216 | tf_op jit(solution)/shard_map/all_to_all | solution.py:104
  111.4 0.9 fusion.117
  112.8 2.0 %reduce.13 = f32[8,6144]{1,0:T(8,128)S(1)} reduce(f32[8,1,6144]{2,1,0:T(1,128)} %copy-done, f32[]{:T(128)} %broadcast.702), dimensions={1}, to_apply=%all_to_all.58.reduce_sub_computation | reduce | bytes 393220 | tf_op jit(solution)/shard_map/all_to_all | solution.py:112
  114.9 3.7 %reshape.593 = f32[1536,1,4,8]{3,2,1,0:T(4,128)S(1)} reshape(f32[8,6144]{1,0:T(8,128)S(1)} %reduce.13) | data formatting | bytes 393216
  118.6 2.0 %copy.198 = f32[1,4,8,8,192]{4,2,3,1,0:T(8,128)S(1)} copy(f32[1,4,8,8,192]{2,1,4,3,0:T(4,128)S(1)} %bitcast.581) | data formatting | bytes 393216 | tf_op jit(solution)/shard_map/all_to_all | solution.py:112
  121.5 2.0 %reduce.12 = f32[8,6144]{1,0:T(8,128)S(1)} reduce(f32[8,1,6144]{2,1,0:T(1,128)} %all-to-all-done, f32[]{:T(128)} %broadcast.702), dimensions={1}, to_apply=%all_to_all.50.reduce_sub_computation | reduce | bytes 393220 | tf_op jit(solution)/shard_map/all_to_all | solution.py:104
  123.6 3.7 %reshape.595 = f32[1536,1,4,8]{3,2,1,0:T(4,128)S(1)} reshape(f32[8,6144]{1,0:T(8,128)S(1)} %reduce.12) | data formatting | bytes 393216
  127.3 2.0 %copy.196 = f32[1,4,8,8,192]{4,2,3,1,0:T(8,128)S(1)} copy(f32[1,4,8,8,192]{2,1,4,3,0:T(4,128)S(1)} %bitcast.582) | data formatting | bytes 393216 | tf_op jit(solution)/shard_map/all_to_all | solution.py:104
  129.6 1.8 gather_fusion.1
  134.4 2.0 %scatter_fusion.1 = f32[4,64,192]{2,0,1:T(4,128)S(1)} fusion(f32[4,64,192]{2,0,1:T(4,128)S(1)} %broadcast.570.clone, s32[48]{0:T(128)S(1)} %copy-done.11, f32[48,4,192]{2,1,0:T(4,128)S(1)} %copy.174), kind=kCustom, calls=%fused_computation.3 | custom fusion | bytes 442560 | tf_op jit(solution)/shard_map/scatter | solution.py:99
  136.3 13.8 %all_to_all.69 = f32[1,4,64,192]{3,1,0,2:T(4,128)S(1)} all-to-all(f32[1,4,64,192]{3,1,0,2:T(4,128)S(1)} %bitcast.583), channel_id=1, replica_groups=mesh['sub'=8,'mem'=4] {'sub'}, dimensions={2} | all-to-all | bytes 393216 | tf_op jit(solution)/shard_map/all_to_all | solution.py:111
  150.4 1.0 convert_multiply_fusion
  152.2 5.0 %scatter_fusion = f32[4,64,192]{2,0,1:T(4,128)} fusion(f32[4,64,192]{2,0,1:T(4,128)} %broadcast.570.clone.1, s32[48]{0:T(128)S(1)} %copy-done.11, f32[48,4,192]{2,1,0:T(4,128)S(1)} %copy.162), kind=kCustom, calls=%fused_computation.2 | custom fusion | bytes 442560 | tf_op jit(solution)/shard_map/scatter | solution.py:99
  157.2 3.4 %all-to-all-start.1 = ((f32[1,4,64,192]{3,1,0,2:T(4,128)}), f32[1,4,64,192]{3,1,0,2:T(4,128)S(1)}, u32[]{:S(2)}, u32[]{:S(2)}) async-start(f32[1,4,64,192]{3,1,0,2:T(4,128)} %bitcast.49), calls=%async_computation.1 | async-start | bytes 524288 | tf_op jit(solution)/shard_map/all_to_all | solution.py:103
  160.7 8.2 %all-to-all-done.1 = f32[1,4,64,192]{3,1,0,2:T(4,128)S(1)} async-done(((f32[1,4,64,192]{3,1,0,2:T(4,128)}), f32[1,4,64,192]{3,1,0,2:T(4,128)S(1)}, u32[]{:S(2)}, u32[]{:S(2)}) %all-to-all-start.1) | async-done | bytes 196640 | tf_op jit(solution)/shard_map/all_to_all | solution.py:103
  169.1 15.7 %all-reduce.2.cloned.1.call-done = f32[4,4,8,1536]{3,2,1,0:T(8,128)} async-done(((f32[4,4,8,1536]{3,2,1,0:T(8,128)}), f32[4,4,8,1536]{3,2,1,0:T(8,128)}) %all-reduce.2.cloned.1.call-update) | async-done | bytes 786448 | tf_op jit(solution)/shard_map/psum | solution.py:120
  184.8 1.7 multiply_add_fusion
  (600 shorter events, 75.5 us)
Async XLA Ops:
  6.5 7.6 %copy-start.3 = (f32[1,4,8,1536]{3,2,1,0:T(8,128)S(1)}, f32[1,4,8,1536]{3,2,1,0:T(8,128)}, u32[]{:S(2)}) copy-start(f32[1,4,8,1536]{3,2,1,0:T(8,128)} %param.17) | copy-start | bytes 589828
  6.5 7.6 %copy-start.4 = (f32[1,4,8,1536]{3,2,1,0:T(8,128)S(1)}, f32[1,4,8,1536]{3,2,1,0:T(8,128)}, u32[]{:S(2)}) copy-start(f32[1,4,8,1536]{3,2,1,0:T(8,128)} %param.18) | copy-start | bytes 589828
  8.0 93.0 %copy-start.7 = (f32[4]{0:T(128)}, f32[4]{0:T(128)S(1)}, u32[]{:S(2)}) copy-start(f32[4]{0:T(128)S(1)} %get-tuple-element.973) | copy-start | bytes 52
  53.8 50.2 %all-to-all-start.2 = ((f32[8,1,6144]{2,1,0:T(1,128)}), f32[8,1,6144]{2,1,0:T(1,128)S(1)}, u32[]{:S(2)}, u32[]{:S(2)}) async-start(f32[8,1,6144]{2,1,0:T(1,128)} %reshape.592), calls=%async_computation.2 | async-start | bytes 393216 | tf_op jit(solution)/shard_map/all_to_all | solution.py:112
  62.4 0.7 copy-start.14
  95.5 4.4 %copy-start.13 = (f32[48]{0:T(128)S(1)}, f32[48]{0:T(128)}, u32[]{:S(2)}) copy-start(f32[48]{0:T(128)} %add_negate_fusion) | copy-start | bytes 580
  95.5 4.4 %copy-start.2 = (f32[48,48]{1,0:T(8,128)S(1)}, f32[48,48]{1,0:T(8,128)}, u32[]{:S(2)}) copy-start(f32[48,48]{1,0:T(8,128)} %maximum_negate_fusion.1) | copy-start | bytes 27652
  95.5 4.4 %copy-start.8 = (f32[4]{0:T(128)S(1)}, f32[4]{0:T(128)}, u32[]{:S(2)}) copy-start(f32[4]{0:T(128)} %get-tuple-element.972) | copy-start | bytes 52
  95.5 7.0 %copy-start.15 = (s32[48]{0:T(128)S(1)}, s32[48]{0:T(128)}, u32[]{:S(2)}) copy-start(s32[48]{0:T(128)} %copy-done.14) | copy-start | bytes 580
  95.5 7.0 %copy-start.16 = (s32[48]{0:T(128)S(1)}, s32[48]{0:T(128)}, u32[]{:S(2)}) copy-start(s32[48]{0:T(128)} %select_reduce_fusion) | copy-start | bytes 580
  104.0 8.3 %copy-start = (f32[8,1,6144]{2,1,0:T(1,128)}, f32[8,1,6144]{2,1,0:T(1,128)S(1)}, u32[]{:S(2)}) copy-start(f32[8,1,6144]{2,1,0:T(1,128)S(1)} %all-to-all-done.2) | copy-start | bytes 589828
  104.0 17.6 %all-to-all-start = ((f32[8,1,6144]{2,1,0:T(1,128)}), f32[8,1,6144]{2,1,0:T(1,128)}, u32[]{:S(2)}, u32[]{:S(2)}) async-start(f32[8,1,6144]{2,1,0:T(1,128)} %reshape.594), calls=%async_computation | async-start | bytes 393216 | tf_op jit(solution)/shard_map/all_to_all | solution.py:104
  110.0 74.8 %all-reduce.2.cloned.1.call-start = ((), (), s32[]{:S(2)}) async-start(), calls=%async_computation.4 | async-start | bytes 1572864 | tf_op jit(solution)/shard_map/psum | solution.py:120
  127.3 4.8 %copy-start.10 = (pred[48]{0:T(512)(128)(4,1)S(1)}, pred[48]{0:T(512)(128)(4,1)}, u32[]{:S(2)}) copy-start(pred[48]{0:T(512)(128)(4,1)} %get-tuple-element.914) | copy-start | bytes 148
  127.3 5.0 %copy-start.5 = (f32[4,48]{1,0:T(4,128)S(1)}, f32[4,48]{1,0:T(4,128)}, u32[]{:S(2)}) copy-start(f32[4,48]{1,0:T(4,128)} %broadcast_multiply_fusion.2) | copy-start | bytes 2308
  127.3 5.0 %copy-start.6 = (f32[4,48]{1,0:T(4,128)S(1)}, f32[4,48]{1,0:T(4,128)}, u32[]{:S(2)}) copy-start(f32[4,48]{1,0:T(4,128)} %broadcast_multiply_fusion.1) | copy-start | bytes 2308
  129.4 4.7 %copy-start.9 = (f32[4]{0:T(128)S(1)}, f32[4]{0:T(128)}, u32[]{:S(2)}) copy-start(f32[4]{0:T(128)} %get-tuple-element.971) | copy-start | bytes 52
  131.3 3.0 %copy-start.11 = (s32[48]{0:T(128)S(1)}, s32[48]{0:T(128)}, u32[]{:S(2)}) copy-start(s32[48]{0:T(128)} %fusion.155) | copy-start | bytes 580
  132.8 17.6 %copy-start.1 = (bf16[1,4,4,8,1536]{4,3,2,1,0:T(8,128)(2,1)S(1)}, bf16[1,4,4,8,1536]{4,3,2,1,0:T(8,128)(2,1)}, u32[]{:S(2)}) copy-start(bf16[1,4,4,8,1536]{4,3,2,1,0:T(8,128)(2,1)} %param.19) | copy-start | bytes 1179652
  136.3 48.5 %copy-start.12 = (f32[1,4]{1,0:T(1,128)S(1)}, f32[1,4]{1,0:T(1,128)}, u32[]{:S(2)}) copy-start(f32[1,4]{1,0:T(1,128)} %param.20) | copy-start | bytes 52
  157.2 11.6 %all-to-all-start.1 = ((f32[1,4,64,192]{3,1,0,2:T(4,128)}), f32[1,4,64,192]{3,1,0,2:T(4,128)S(1)}, u32[]{:S(2)}, u32[]{:S(2)}) async-start(f32[1,4,64,192]{3,1,0,2:T(4,128)} %bitcast.49), calls=%async_computation.1 | async-start | bytes 524288 | tf_op jit(solution)/shard_map/all_to_all | solution.py:103
Sparse Core Ops, SparseCore 0:
  151.5 33.2 all-reduce.1
where the time goes:
time: 194 us; the launch traced here: 193 us
  local copies, waits for them, and re-layouts  61.2 us (32%)
  matrix products  41 us (21%)
  waiting for transfers between devices  23.9 us (12%)
  other arithmetic  21 us (11%)
  starting transfers between devices  16.9 us (9%)
  between operations  14.1 us (7%)
  blocking collectives  13.8 us (7%)
    dot_general x52, matrix products, advance(): jnp.einsum('blrj,lij->blri', current, full_power, precision=lax.Precision...  27.5 us
    unnamed x40, local copies, waits for them, and re-layouts  17.7 us
    psum x1, waiting for transfers between devices, body(): summed = lax.psum(partial_sum, 'mem')  15.7 us
    all_to_all x1, blocking collectives, body(): lax.all_to_all(column_filter(lax.all_to_all(member_x, 'sub', split_axis=3...  13.8 us
    while x144, local copies, waits for them, and re-layouts  10.3 us
    all_to_all x1, waiting for transfers between devices, body(): lax.all_to_all(column_filter(lax.all_to_all(static_x, 'sub', split_axis=3...  8.16 us
    dot_general x48, matrix products, advance(): jnp.einsum('blrj,lkj->blrk', current, last_rows, precision=lax.Precision....  8.15 us
    slice x48, local copies, waits for them, and re-layouts, advance(): finals.append(output[..., -1])  7.58 us
  transfers between devices with their start and end apart: 4, of which 2 were waited for; matrix products, arithmetic and copies ran while one was open for 31% of the time, Pallas kernels for 0%

commit v1 on v0

--- a/solution.py
+++ b/solution.py
@@ -1,8 +1,11 @@
+import functools
 import math
 
 import jax
 import jax.numpy as jnp
 from jax import lax
+from jax.experimental import pallas as pl
+from jax.experimental.pallas import tpu as pltpu
 from jax.sharding import PartitionSpec as P
 
 ROWS_DEV = 6
@@ -122,9 +125,241 @@
     return static_scale[:, :, None, None] * static_done + own_sum * (1.0 / math.sqrt(member_count))
 
 
+MESH = pl.DeviceIdType.MESH
+BLK = 128
+
+
+def response(lag, inverse):
+    decay = jnp.exp(-inverse)
+    gain = (1.0 - decay) * (1.0 - decay)
+    gain = gain * gain * (1.0 / 6.0)
+    poly = (lag + 1.0) * (lag + 2.0) * (lag + 3.0)
+    value = gain * poly * jnp.exp(-jnp.maximum(lag, 0.0) * inverse)
+    return jnp.where(lag >= 0.0, value, 0.0)
+
+
+def split(values):
+    high = values.astype(jnp.bfloat16)
+    low = (values - high.astype(jnp.float32)).astype(jnp.bfloat16)
+    return high, low
+
+
+def banded(blocks, weights):
+    rows = 8 * len(blocks)
+    high, low = split(jnp.concatenate(blocks, axis=0))
+    both = jnp.concatenate([high, low], axis=0)
+    prod = jnp.dot(both, weights, preferred_element_type=jnp.float32)
+    total = prod[:rows, :BLK] + (prod[:rows, BLK:] + prod[rows:, :BLK])
+    return [total[8 * b : 8 * b + 8] for b in range(len(blocks))]
+
+
+def smooth_x(row_values, ahead, back):
+    count = row_values.shape[1] // BLK
+    zero = jnp.zeros((8, BLK), jnp.float32)
+    cells = [zero] + [row_values[:, b * BLK : (b + 1) * BLK] for b in range(count)]
+    cells = banded([jnp.concatenate(cells[b : b + 2], axis=1) for b in range(count)], ahead) + [zero]
+    return banded([jnp.concatenate(cells[b : b + 2], axis=1) for b in range(count)], back)
+
+
+def kernel(
+    subs, levels, static_ref, alpha_ref, pert_ref, scale_ref, lx_ref, ly_ref, len_ref, out_ref,
+    ahead, back, outgo, income, result, done, part, fold, give, take,
+    send1, recv1, send2, recv2, send3, recv3, send4, recv4,
+):
+    me = lax.axis_index("sub")
+    mem = lax.axis_index("mem")
+    side = lax.rem(mem, 2)
+    near = mem + 1 - 2 * side
+    far = lax.rem(mem + 2, 4)
+    pieces = subs // levels
+    width = static_ref.shape[2] // pieces
+    per_piece = width // BLK
+
+    barrier = pltpu.get_barrier_semaphore()
+    for step in range(1, subs):
+        pl.semaphore_signal(
+            barrier, inc=1, device_id=(lax.rem(me + step, subs), mem), device_id_type=MESH
+        )
+    for other in (near, far):
+        pl.semaphore_signal(barrier, inc=1, device_id=(me, other), device_id_type=MESH)
+
+    at_in = lax.broadcasted_iota(jnp.int32, (2 * BLK, BLK), 0)
+    at_out = lax.broadcasted_iota(jnp.int32, (2 * BLK, BLK), 1)
+    lag_ahead = (at_out + BLK - at_in).astype(jnp.float32)
+    lag_back = (at_in - at_out).astype(jnp.float32)
+    for level in range(levels):
+        inverse = 1.0 / jnp.full((1, BLK), lx_ref[level], jnp.float32)
+        for ref, lag in ((ahead, lag_ahead), (back, lag_back)):
+            high, low = split(response(lag, inverse))
+            ref[level, :, :BLK] = high
+            ref[level, :, BLK:] = low
+
+    slot = lax.broadcasted_iota(jnp.int32, (8, static_ref.shape[2]), 0)
+    valid = slot < len_ref[me]
+
+    def exchange(src, dst, sends, recvs, field, step):
+        other = lax.rem(me + step, subs)
+        return pltpu.make_async_remote_copy(
+            src_ref=src.at[field, other],
+            dst_ref=dst.at[field, me],
+            send_sem=sends.at[field, step],
+            recv_sem=recvs.at[field, me],
+            device_id=(other, mem),
+            device_id_type=MESH,
+        )
+
+    def arrival(src, dst, sends, recvs, field, step):
+        other = lax.rem(me + step, subs)
+        return pltpu.make_async_remote_copy(
+            src_ref=src.at[field, other],
+            dst_ref=dst.at[field, other],
+            send_sem=sends.at[field, step],
+            recv_sem=recvs.at[field, other],
+            device_id=(other, mem),
+            device_id_type=MESH,
+        )
+
+    for field, ref in ((0, alpha_ref), (1, static_ref)):
+        for level in range(levels):
+            cells = smooth_x(jnp.where(valid, ref[level], 0.0), ahead[level], back[level])
+            for piece in range(pieces):
+                outgo[field, level * pieces + piece] = jnp.concatenate(
+                    cells[piece * per_piece : (piece + 1) * per_piece], axis=1
+                )
+        if field == 0:
+            pl.semaphore_wait(barrier, subs + 1)
+        for step in range(1, subs):
+            exchange(outgo, income, send1, recv1, field, step).start()
+        income[field, me] = outgo[field, me]
+
+    slots = subs * 8
+    row = lax.broadcasted_iota(jnp.int32, (slots, slots), 0)
+    col = lax.broadcasted_iota(jnp.int32, (slots, slots), 1)
+    row_owner, col_owner = row // 8, col // 8
+    row_at, col_at = row - 8 * row_owner, col - 8 * col_owner
+    row_pos, col_pos, row_len, col_len = row_at, col_at, row * 0, col * 0
+    start = 0
+    for owner in range(subs):
+        held = len_ref[owner]
+        row_pos = row_pos + jnp.where(row_owner == owner, start, 0)
+        col_pos = col_pos + jnp.where(col_owner == owner, start, 0)
+        row_len = row_len + jnp.where(row_owner == owner, held, 0)
+        col_len = col_len + jnp.where(col_owner == owner, held, 0)
+        start = start + held
+    real = jnp.logical_and(row_at < row_len, col_at < col_len)
+    lag = (row_pos - col_pos).astype(jnp.float32)
+    mine = me // pieces
+    len_x = jnp.full((1, slots), lx_ref[mine], jnp.float32)
+    len_y = jnp.full((1, slots), ly_ref[mine], jnp.float32)
+    inverse = 1.0 / len_y
+    lower = jnp.where(real, response(lag, inverse), 0.0)
+    upper = jnp.where(real, response(-lag, inverse), 0.0)
+    mixed = jnp.dot(
+        upper, lower, precision=lax.Precision.HIGHEST, preferred_element_type=jnp.float32
+    ) * jnp.sqrt(len_x * len_y)
+    mix_high, mix_low = split(mixed)
+
+    for field in range(2):
+        for step in range(1, subs):
+            arrival(outgo, income, send1, recv1, field, step).wait_recv()
+        high, low = split(income[field].reshape(slots, width))
+        mixed_rows = jnp.dot(mix_high, high, preferred_element_type=jnp.float32) + (
+            jnp.dot(mix_low, high, preferred_element_type=jnp.float32)
+            + jnp.dot(mix_high, low, preferred_element_type=jnp.float32)
+        )
+        result[field] = mixed_rows.reshape(subs, 8, width)
+        for step in range(1, subs):
+            exchange(result, done, send2, recv2, field, step).start()
+        done[field, me] = result[field, me]
+
+    for step in range(1, subs):
+        arrival(result, done, send2, recv2, 0, step).wait_recv()
+
+    def weight_rows():
+        return [
+            jnp.concatenate([done[0, level * pieces + piece] for piece in range(pieces)], axis=1)
+            for level in range(levels)
+        ]
+
+    weights = jnp.concatenate(weight_rows(), axis=0)
+    for half in range(2):
+        variable = 2 * half + 1 - side
+        part[half] = pert_ref[variable].astype(jnp.float32) * weights
+    to_near = pltpu.make_async_remote_copy(
+        src_ref=part, dst_ref=fold, send_sem=send3.at[0], recv_sem=recv3.at[0],
+        device_id=(me, near), device_id_type=MESH,
+    )
+    to_near.start()
+    top = mem // 2
+    own = pert_ref[2 * top + side].astype(jnp.float32) * weights
+    passed = pert_ref[2 * (1 - top) + side].astype(jnp.float32) * weights
+    to_near.wait_recv()
+    give[...] = passed + fold[1 - top]
+    to_far = pltpu.make_async_remote_copy(
+        src_ref=give, dst_ref=take, send_sem=send4.at[0], recv_sem=recv4.at[0],
+        device_id=(me, far), device_id_type=MESH,
+    )
+    to_far.start()
+    own = own + fold[top]
+    for step in range(1, subs):
+        arrival(result, done, send2, recv2, 1, step).wait_recv()
+    to_far.wait_recv()
+    total = (own + take[...]) * 0.5
+    for level in range(levels):
+        fixed = jnp.concatenate(
+            [done[1, level * pieces + piece] for piece in range(pieces)], axis=1
+        )
+        out_ref[level] = scale_ref[0, level] * fixed + total[8 * level : 8 * level + 8]
+    for field in range(2):
+        for step in range(1, subs):
+            exchange(outgo, income, send1, recv1, field, step).wait_send()
+            exchange(result, done, send2, recv2, field, step).wait_send()
+    to_near.wait_send()
+    to_far.wait_send()
+
+
+def fused(static_control, alpha_field, perturbations, static_scale, length_x, length_y, lengths):
+    subs = lax.axis_size("sub")
+    unused, levels, rows, cells = static_control.shape
+    variables = perturbations.shape[1]
+    width = cells // (subs // levels)
+    vmem = pl.BlockSpec(memory_space=pltpu.VMEM)
+    smem = pl.BlockSpec(memory_space=pltpu.SMEM)
+    swap = pltpu.VMEM((2, subs, rows, width), jnp.float32)
+    flat = (levels * rows, cells)
+    out = pl.pallas_call(
+        functools.partial(kernel, subs, levels),
+        out_shape=jax.ShapeDtypeStruct((levels, rows, cells), jnp.float32),
+        in_specs=[vmem] * 3 + [smem] * 4,
+        out_specs=vmem,
+        scratch_shapes=[
+            pltpu.VMEM((levels, 2 * BLK, 2 * BLK), jnp.bfloat16),
+            pltpu.VMEM((levels, 2 * BLK, 2 * BLK), jnp.bfloat16),
+            swap, swap, swap, swap,
+            pltpu.VMEM((2,) + flat, jnp.float32),
+            pltpu.VMEM((2,) + flat, jnp.float32),
+            pltpu.VMEM(flat, jnp.float32),
+            pltpu.VMEM(flat, jnp.float32),
+        ]
+        + [pltpu.SemaphoreType.DMA((2, subs))] * 4
+        + [pltpu.SemaphoreType.DMA((1,))] * 4,
+        compiler_params=pltpu.CompilerParams(
+            collective_id=0, has_side_effects=True, vmem_limit_bytes=32 * 1024 * 1024
+        ),
+    )(
+        static_control[0], alpha_field[0], perturbations.reshape((variables,) + flat),
+        static_scale, length_x, length_y, lengths,
+    )
+    return out[None]
+
+
+def fits(mesh):
+    return mesh.shape["sub"] == 8 and mesh.shape["mem"] == 4
+
+
 def solution(mesh):
     return jax.shard_map(
-        body,
+        fused if fits(mesh) else body,
         mesh=mesh,
         in_specs=(
             P("mem", None, "sub", None),

time: 194 us -> 33.3 us (0.17)
  local copies, waits for them, and re-layouts: 61.2 us -> 4.23 us
  matrix products: 41 us -> 0 us
  Pallas kernels: 0 us -> 28.8 us
  waiting for transfers between devices: 23.9 us -> 0 us
  other arithmetic: 21 us -> 0 us
  starting transfers between devices: 16.9 us -> 0 us
  between operations: 14.1 us -> 0.02 us
  blocking collectives: 13.8 us -> 0 us
    dot_general x110 -> x0, matrix products: 41 us -> none  [the longest x52 27.5 us: advance(): jnp.einsum('blrj,lij->blri', current, full_power, precision=lax.Precision...]
    pallas_call x0 -> x1, Pallas kernels: none -> 28.8 us  [fused(): pl.pallas_call(functools.partial(kernel, subs, levels), out_shape=jax.Sha...]
    all_to_all x3 -> x0, starting transfers between devices: 16.7 us -> none  [the longest x1 7.28 us: body(): lax.all_to_all(member_x, 'sub', split_axis=3, concat_axis=2, tiled=True)]
    psum x1 -> x0, waiting for transfers between devices: 15.7 us -> none  [body(): summed = lax.psum(partial_sum, 'mem')]
    all_to_all x1 -> x0, blocking collectives: 13.8 us -> none  [body(): lax.all_to_all(column_filter(lax.all_to_all(member_x, 'sub', split_axis=3...]
    unnamed x40 -> x15, local copies, waits for them, and re-layouts: 17.7 us -> 4.23 us
    while x144 -> x0, local copies, waits for them, and re-layouts: 10.3 us -> none
    all_to_all x3 -> x0, waiting for transfers between devices: 8.16 us -> none  [the longest x1 8.16 us: body(): lax.all_to_all(column_filter(lax.all_to_all(static_x, 'sub', split_axis=3...]
  transfers between devices with their start and end apart: 4 -> 0, of which waited for: 2 -> 0; matrix products, arithmetic and copies ran while one was open for 31% -> 0% of each run, Pallas kernels for 0% -> 0%
where the time goes in v1:
time: 33.3 us; the launch traced here: 33.1 us
  Pallas kernels  28.8 us (86%)
  local copies, waits for them, and re-layouts  4.23 us (13%)
    pallas_call x1, Pallas kernels, fused(): pl.pallas_call(functools.partial(kernel, subs, levels), out_shape=jax.Sha...  28.8 us
    unnamed x15, local copies, waits for them, and re-layouts  4.23 us

profile of v1, /device:TPU:0, one launch (start us, length us, event | category | flops | bytes accessed | tf_op | source)
XLA Modules:
  0.0 33.1 jit_solution(8015871335774709297)
XLA Ops:
  0.0 0.0 copy-start.6
  0.0 0.0 copy-start.3
  0.0 0.0 copy-start.4
  0.0 0.0 copy-start.5
  0.0 0.6 %copy-done.6 = s32[8]{0:T(128)S(1)} copy-done((s32[8]{0:T(128)S(1)}, s32[8]{0:T(128)}, u32[]{:S(2)}) %copy-start.6) | copy-done | bytes 56
  0.7 0.0 copy-done.3
  0.7 0.0 copy-done.4
  0.7 0.0 copy-done.5
  0.7 0.0 copy-start
  0.7 1.0 %copy-done = bf16[1,4,4,8,1536]{4,3,2,1,0:T(8,128)(2,1)S(1)} copy-done((bf16[1,4,4,8,1536]{4,3,2,1,0:T(8,128)(2,1)S(1)}, bf16[1,4,4,8,1536]{4,3,2,1,0:T(8,128)(2,1)}, u32[]{:S(2)}) %copy-start) | copy-done | bytes 393240
  1.7 0.0 copy-start.1
  1.7 0.9 %copy-done.1 = f32[1,4,8,1536]{3,2,1,0:T(8,128)S(1)} copy-done((f32[1,4,8,1536]{3,2,1,0:T(8,128)S(1)}, f32[1,4,8,1536]{3,2,1,0:T(8,128)}, u32[]{:S(2)}) %copy-start.1) | copy-done | bytes 196632
  2.6 0.0 copy-start.2
  2.6 0.9 %copy-done.2 = f32[1,4,8,1536]{3,2,1,0:T(8,128)S(1)} copy-done((f32[1,4,8,1536]{3,2,1,0:T(8,128)S(1)}, f32[1,4,8,1536]{3,2,1,0:T(8,128)}, u32[]{:S(2)}) %copy-start.2) | copy-done | bytes 196632
  3.6 28.8 %shard_map.73 = f32[4,8,1536]{2,1,0:T(8,128)S(1)} custom-call(f32[4,8,1536]{2,1,0:T(8,128)S(1)} %bitcast.6, f32[4,8,1536]{2,1,0:T(8,128)S(1)} %bitcast.7, bf16[4,32,1536]{2,1,0:T(8,128)(2,1)S(1)} %bitcast.5, f32[1,4]{1,0:T(1,128)S(1)} %copy-done.3, f32[4]{0:T(128)S(1)} %copy-done.4, f32[4]{0:T(128)S(1)} %copy-done.5, s32[8]{0:T(128)S(1)} %copy-done.6), custom_call_target="tpu_custom_call" | custom-call | tf_op jit(solution)/shard_map/pallas_call | solution.py:330
  32.4 0.7 %copy.9 = f32[1,4,8,1536]{3,2,1,0:T(8,128)} copy(f32[1,4,8,1536]{3,2,1,0:T(8,128)S(1)} %bitcast.4) | data formatting | bytes 393216
Async XLA Ops:
  0.0 0.7 %copy-start.6 = (s32[8]{0:T(128)S(1)}, s32[8]{0:T(128)}, u32[]{:S(2)}) copy-start(s32[8]{0:T(128)} %len_ref.1) | copy-start | bytes 100
  0.0 0.7 %copy-start.3 = (f32[1,4]{1,0:T(1,128)S(1)}, f32[1,4]{1,0:T(1,128)}, u32[]{:S(2)}) copy-start(f32[1,4]{1,0:T(1,128)} %scale_ref.1) | copy-start | bytes 52
  0.0 0.7 %copy-start.4 = (f32[4]{0:T(128)S(1)}, f32[4]{0:T(128)}, u32[]{:S(2)}) copy-start(f32[4]{0:T(128)} %lx_ref.1) | copy-start | bytes 52
  0.0 0.7 %copy-start.5 = (f32[4]{0:T(128)S(1)}, f32[4]{0:T(128)}, u32[]{:S(2)}) copy-start(f32[4]{0:T(128)} %ly_ref.1) | copy-start | bytes 52
  0.7 1.0 %copy-start = (bf16[1,4,4,8,1536]{4,3,2,1,0:T(8,128)(2,1)S(1)}, bf16[1,4,4,8,1536]{4,3,2,1,0:T(8,128)(2,1)}, u32[]{:S(2)}) copy-start(bf16[1,4,4,8,1536]{4,3,2,1,0:T(8,128)(2,1)} %param.9) | copy-start | bytes 1179652
  1.7 0.9 %copy-start.1 = (f32[1,4,8,1536]{3,2,1,0:T(8,128)S(1)}, f32[1,4,8,1536]{3,2,1,0:T(8,128)}, u32[]{:S(2)}) copy-start(f32[1,4,8,1536]{3,2,1,0:T(8,128)} %param.7) | copy-start | bytes 589828
  2.6 0.9 %copy-start.2 = (f32[1,4,8,1536]{3,2,1,0:T(8,128)S(1)}, f32[1,4,8,1536]{3,2,1,0:T(8,128)}, u32[]{:S(2)}) copy-start(f32[1,4,8,1536]{3,2,1,0:T(8,128)} %param.8) | copy-start | bytes 589828

commit v2 on v0

--- a/solution.py
+++ b/solution.py
@@ -1,8 +1,11 @@
+import functools
 import math
 
 import jax
 import jax.numpy as jnp
 from jax import lax
+from jax.experimental import pallas as pl
+from jax.experimental.pallas import tpu as pltpu
 from jax.sharding import PartitionSpec as P
 
 ROWS_DEV = 6
@@ -122,9 +125,396 @@
     return static_scale[:, :, None, None] * static_done + own_sum * (1.0 / math.sqrt(member_count))
 
 
+MESH = pl.DeviceIdType.MESH
+BLK = 128
+HIGHEST = lax.Precision.HIGHEST
+
+
+def taps(lag, depth, inverse):
+    rest = 1.0 - jnp.exp(-inverse)
+    value = jnp.exp(-jnp.maximum(lag, 0.0) * inverse)
+    for order in range(1, 4):
+        factor = rest * (lag + float(order)) * (1.0 / order)
+        if isinstance(depth, int):
+            value = value * factor if depth >= order else value
+        else:
+            value = value * jnp.where(depth >= order, factor, 1.0)
+    return jnp.where(lag >= 0.0, value, 0.0)
+
+
+def passed(lag, depth, inverse):
+    return taps(lag, depth, inverse) * (1.0 - jnp.exp(-inverse))
+
+
+def split(values):
+    high = values.astype(jnp.bfloat16)
+    low = (values - high.astype(jnp.float32)).astype(jnp.bfloat16)
+    return high, low
+
+
+def product(matrix, values):
+    mat_high, mat_low = matrix
+    high, low = split(values)
+    return jnp.dot(mat_high, high, preferred_element_type=jnp.float32) + (
+        jnp.dot(mat_low, high, preferred_element_type=jnp.float32)
+        + jnp.dot(mat_high, low, preferred_element_type=jnp.float32)
+    )
+
+
+def banded(blocks, weights):
+    rows = 8 * len(blocks)
+    high, low = split(jnp.concatenate(blocks, axis=0))
+    both = jnp.concatenate([high, low], axis=0)
+    prod = jnp.dot(both, weights, preferred_element_type=jnp.float32)
+    total = prod[:rows, :BLK] + (prod[:rows, BLK:] + prod[rows:, :BLK])
+    return [total[8 * b : 8 * b + 8] for b in range(len(blocks))]
+
+
+def smooth_x(row_values, ahead, back):
+    count = row_values.shape[1] // BLK
+    zero = jnp.zeros((8, BLK), jnp.float32)
+    cells = [zero] + [row_values[:, b * BLK : (b + 1) * BLK] for b in range(count)]
+    cells = banded([jnp.concatenate(cells[b : b + 2], axis=1) for b in range(count)], ahead) + [zero]
+    return banded([jnp.concatenate(cells[b : b + 2], axis=1) for b in range(count)], back)
+
+
+def choose(index, options):
+    value = options[0]
+    for which in range(1, len(options)):
+        value = jnp.where(index == which, options[which], value)
+    return value
+
+
+def line_matrices(group, groups, levels, lx_ref, ly_ref, len_ref):
+    subs = 2 * groups
+    held = [len_ref[sub] for sub in range(subs)]
+    starts = [jnp.int32(0)]
+    for sub in range(subs):
+        starts.append(starts[-1] + held[sub])
+    edges = [starts[2 * g] for g in range(groups + 1)]
+
+    def iota(shape, axis):
+        return lax.broadcasted_iota(jnp.int32, shape, axis)
+
+    def own_slots(index):
+        sub = 2 * group + index // 32
+        slot = index % 8
+        where = choose(sub, starts[:subs]) + slot
+        real = slot < choose(sub, held)
+        return where.astype(jnp.float32), real, (index // 8) % 4
+
+    def scale_of(level, ref):
+        return choose(level, [ref[lev] for lev in range(levels)])
+
+    rows = 16 * levels
+    slots = 8 * subs
+    far_cols = (groups - 1) * 4 * levels
+    row_at, row_real, row_level = own_slots(iota((rows, 1), 0))
+    col_at, col_real, col_level = own_slots(iota((1, rows), 1))
+    row_len = scale_of(row_level, ly_ref) + jnp.zeros((rows, 1), jnp.float32)
+    row_inv = 1.0 / row_len
+    col_inv = 1.0 / (scale_of(col_level, ly_ref) + jnp.zeros((1, rows), jnp.float32))
+
+    def all_slots(index):
+        sub, slot = index // 8, index % 8
+        where = choose(sub, starts[:subs]) + slot
+        return where.astype(jnp.float32), slot < choose(sub, held)
+
+    k_col_at, k_col_real = all_slots(iota((slots, 1), 0))
+    k_row_at, k_row_real = all_slots(iota((1, slots), 1))
+
+    far = iota((1, far_cols), 1)
+    far_step = far // (4 * levels) + 1
+    far_level = (far // 4) % levels
+    far_state = far % 4
+    far_group = far_step * -1 + group
+    far_group = jnp.where(far_group < 0, far_group + groups, far_group)
+    far_inv = 1.0 / (scale_of(far_level, ly_ref) + jnp.zeros((1, far_cols), jnp.float32))
+    far_before = far_group < group
+    far_first = choose(far_group, edges[:groups]).astype(jnp.float32)
+    far_end = choose(far_group, edges[1:]).astype(jnp.float32)
+    far_depth = 3 - far_state
+    far_decay = jnp.exp(-far_inv)
+
+    forward = jnp.where(
+        jnp.logical_and(k_col_real, col_real), passed(k_col_at - col_at, 3, col_inv), 0.0
+    )
+    entry = jnp.where(
+        k_col_real, taps(k_col_at - far_end, far_depth, far_inv) * far_decay, 0.0
+    )
+    backward = jnp.where(
+        jnp.logical_and(row_real, k_row_real), passed(k_row_at - row_at, 3, row_inv), 0.0
+    )
+    inner = jnp.dot(backward, forward, precision=HIGHEST, preferred_element_type=jnp.float32)
+    outer = jnp.dot(backward, entry, precision=HIGHEST, preferred_element_type=jnp.float32)
+    behind = jnp.where(
+        row_real, taps(far_first - 1.0 - row_at, far_depth, far_inv) * far_decay, 0.0
+    )
+    outer = jnp.where(far_before, outer, behind)
+    factor = jnp.sqrt(scale_of(row_level, lx_ref) * row_len)
+    inner = jnp.where(row_level == col_level, inner, 0.0) * factor
+    outer = jnp.where(row_level == far_level, outer, 0.0) * factor
+
+    state_rows = 4 * levels
+    st = iota((state_rows, 1), 0)
+    st_level, st_depth = st // 4, st % 4
+    st_inv = 1.0 / (scale_of(st_level, ly_ref) + jnp.zeros((state_rows, 1), jnp.float32))
+    first = choose(group, edges[:groups]).astype(jnp.float32)
+    end = choose(group, edges[1:]).astype(jnp.float32)
+    leaving = jnp.where(col_real, passed(end - 1.0 - col_at, st_depth, st_inv), 0.0)
+    turned = jnp.where(k_row_real, passed(k_row_at - first, st_depth, st_inv), 0.0)
+    turned = jnp.dot(turned, forward, precision=HIGHEST, preferred_element_type=jnp.float32)
+    moments = [
+        jnp.where(st_level == col_level, part, 0.0) for part in (leaving, turned)
+    ]
+    return jnp.concatenate(moments, axis=0), inner, outer
+
+
+def kernel(
+    groups, levels, static_hbm, alpha_hbm, pert_hbm, scale_ref, lx_ref, ly_ref, len_ref, out_ref,
+    static_ref, alpha_ref, pert_ref, ahead, back, outgo, pair, mom, msg, result, done,
+    part, fold, give, take, own,
+    load, send1, recv1, send2, recv2, send3, recv3, send4, recv4, send5, recv5,
+):
+    me = lax.axis_index("sub")
+    mem = lax.axis_index("mem")
+    group, side = me // 2, lax.rem(me, 2)
+    beside = me + 1 - 2 * side
+    core = lax.rem(mem, 2)
+    near = mem + 1 - 2 * core
+    far = lax.rem(mem + 2, 4)
+    top = mem // 2
+    state_rows = 4 * levels
+    half_rows = 8 * levels
+    width = static_ref.shape[2] // 2
+    per_half = width // BLK
+
+    loads = [
+        pltpu.make_async_copy(src, dst, load.at[which])
+        for which, (src, dst) in enumerate(
+            ((alpha_hbm, alpha_ref), (static_hbm, static_ref), (pert_hbm, pert_ref))
+        )
+    ]
+    for one in loads:
+        one.start()
+
+    barrier = pltpu.get_barrier_semaphore()
+    friends = [(beside, mem), (me, near), (me, far)]
+    for step in range(1, groups):
+        friends.append((2 * lax.rem(group + step, groups) + side, mem))
+    for friend in friends:
+        pl.semaphore_signal(barrier, inc=1, device_id=friend, device_id_type=MESH)
+
+    at_in = lax.broadcasted_iota(jnp.int32, (2 * BLK, BLK), 0)
+    at_out = lax.broadcasted_iota(jnp.int32, (2 * BLK, BLK), 1)
+    lag_ahead = (at_out + BLK - at_in).astype(jnp.float32)
+    lag_back = (at_in - at_out).astype(jnp.float32)
+    for level in range(levels):
+        inverse = 1.0 / jnp.full((1, BLK), lx_ref[level], jnp.float32)
+        for ref, lag in ((ahead, lag_ahead), (back, lag_back)):
+            high, low = split(passed(lag, 3, inverse))
+            ref[level, :, :BLK] = high
+            ref[level, :, BLK:] = low
+
+    slot = lax.broadcasted_iota(jnp.int32, (8, static_ref.shape[2]), 0)
+    valid = slot < len_ref[me]
+
+    def to_pair(field):
+        return pltpu.make_async_remote_copy(
+            src_ref=outgo.at[field, 1 - side], dst_ref=pair.at[field, side],
+            send_sem=send1.at[field], recv_sem=recv1.at[field],
+            device_id=(beside, mem), device_id_type=MESH,
+        )
+
+    def from_pair(field):
+        return pltpu.make_async_remote_copy(
+            src_ref=outgo.at[field, 1 - side], dst_ref=pair.at[field, 1 - side],
+            send_sem=send1.at[field], recv_sem=recv1.at[field],
+            device_id=(beside, mem), device_id_type=MESH,
+        )
+
+    def to_group(field, step):
+        other = lax.rem(group + step, groups)
+        kind = jnp.where(other > group, 0, 1)
+        return pltpu.make_async_remote_copy(
+            src_ref=mom.at[field, kind], dst_ref=msg.at[field, step - 1],
+            send_sem=send2.at[field, step], recv_sem=recv2.at[field, step],
+            device_id=(2 * other + side, mem), device_id_type=MESH,
+        )
+
+    def to_home(field):
+        return pltpu.make_async_remote_copy(
+            src_ref=result.at[field], dst_ref=done.at[field, side],
+            send_sem=send3.at[field], recv_sem=recv3.at[field],
+            device_id=(beside, mem), device_id_type=MESH,
+        )
+
+    def from_home(field):
+        return pltpu.make_async_remote_copy(
+            src_ref=result.at[field], dst_ref=done.at[field, 1 - side],
+            send_sem=send3.at[field], recv_sem=recv3.at[field],
+            device_id=(beside, mem), device_id_type=MESH,
+        )
+
+    def to_near(half):
+        return pltpu.make_async_remote_copy(
+            src_ref=part.at[half], dst_ref=fold.at[half],
+            send_sem=send4.at[half], recv_sem=recv4.at[half],
+            device_id=(me, near), device_id_type=MESH,
+        )
+
+    def to_far(half):
+        return pltpu.make_async_remote_copy(
+            src_ref=give.at[half], dst_ref=take.at[half],
+            send_sem=send5.at[half], recv_sem=recv5.at[half],
+            device_id=(me, far), device_id_type=MESH,
+        )
+
+    for field, ref in ((0, alpha_ref), (1, static_ref)):
+        loads[field].wait()
+        for level in range(levels):
+            cells = smooth_x(jnp.where(valid, ref[level], 0.0), ahead[level], back[level])
+            for half in range(2):
+                outgo[field, half, 8 * level : 8 * level + 8] = jnp.concatenate(
+                    cells[half * per_half : (half + 1) * per_half], axis=1
+                )
+        if field == 0:
+            pl.semaphore_wait(barrier, len(friends))
+        to_pair(field).start()
+        pair[field, side] = outgo[field, side]
+
+    moments, inner, outer = line_matrices(group, groups, levels, lx_ref, ly_ref, len_ref)
+    moments, inner, outer = split(moments), split(inner), split(outer)
+
+    def pair_rows(field):
+        return jnp.concatenate([pair[field, 0], pair[field, 1]], axis=0)
+
+    for field in range(2):
+        from_pair(field).wait_recv()
+        both = product(moments, pair_rows(field))
+        for kind in range(2):
+            mom[field, kind] = both[kind * state_rows : (kind + 1) * state_rows]
+        for step in range(1, groups):
+            to_group(field, step).start()
+
+    def finish(field):
+        mixed = product(inner, pair_rows(field))
+        for step in range(1, groups):
+            to_group(field, step).wait_recv()
+        arrived = jnp.concatenate([msg[field, step] for step in range(groups - 1)], axis=0)
+        mixed = mixed + product(outer, arrived)
+        mine, theirs = mixed[:half_rows], mixed[half_rows:]
+        result[field] = jnp.where(side == 0, theirs, mine)
+        to_home(field).start()
+        done[field, side] = jnp.where(side == 0, mine, theirs)
+
+    def terms(half, variable):
+        columns = pl.ds(pl.multiple_of(half * width, BLK), width)
+        return pert_ref[variable, :, columns].astype(jnp.float32) * done[0, half]
+
+    def gather(half):
+        for which in range(2):
+            part[half, which] = terms(half, 2 * which + 1 - core)
+        to_near(half).start()
+
+    def forward_sum(half):
+        to_near(half).wait_recv()
+        give[half] = terms(half, 2 * (1 - top) + core) + fold[half, 1 - top]
+        to_far(half).start()
+        own[half] = terms(half, 2 * top + core) + fold[half, top]
+
+    finish(0)
+    loads[2].wait()
+    gather(side)
+    forward_sum(side)
+    from_home(0).wait_recv()
+    gather(1 - side)
+    forward_sum(1 - side)
+    finish(1)
+
+    def write(half):
+        to_far(half).wait_recv()
+        total = (own[half] + take[half]) * 0.5
+        columns = pl.ds(pl.multiple_of(half * width, BLK), width)
+        for level in range(levels):
+            rows = slice(8 * level, 8 * level + 8)
+            out_ref[level, :, columns] = (
+                scale_ref[0, level] * done[1, half, rows] + total[rows]
+            )
+
+    write(side)
+    from_home(1).wait_recv()
+    write(1 - side)
+    for field in range(2):
+        to_pair(field).wait_send()
+        to_home(field).wait_send()
+        for step in range(1, groups):
+            to_group(field, step).wait_send()
+    for half in (side, 1 - side):
+        to_near(half).wait_send()
+        to_far(half).wait_send()
+
+
+def fused(static_control, alpha_field, perturbations, static_scale, length_x, length_y, lengths):
+    groups = lax.axis_size("sub") // 2
+    unused, levels, rows, cells = static_control.shape
+    variables = perturbations.shape[1]
+    width = cells // 2
+    flat = (levels * rows, width)
+    anywhere = pl.BlockSpec(memory_space=pl.ANY)
+    smem = pl.BlockSpec(memory_space=pltpu.SMEM)
+
+    def buffer(*shape):
+        return pltpu.VMEM(shape, jnp.float32)
+
+    dma = pltpu.SemaphoreType.DMA
+    out = pl.pallas_call(
+        functools.partial(kernel, groups, levels),
+        out_shape=jax.ShapeDtypeStruct((levels, rows, cells), jnp.float32),
+        in_specs=[anywhere] * 3 + [smem] * 4,
+        out_specs=pl.BlockSpec(memory_space=pltpu.VMEM),
+        scratch_shapes=[
+            buffer(levels, rows, cells),
+            buffer(levels, rows, cells),
+            pltpu.VMEM((variables, levels * rows, cells), jnp.bfloat16),
+            pltpu.VMEM((levels, 2 * BLK, 2 * BLK), jnp.bfloat16),
+            pltpu.VMEM((levels, 2 * BLK, 2 * BLK), jnp.bfloat16),
+            buffer(2, 2, *flat),
+            buffer(2, 2, *flat),
+            buffer(2, 2, 4 * levels, width),
+            buffer(2, groups - 1, 4 * levels, width),
+            buffer(2, *flat),
+            buffer(2, 2, *flat),
+            buffer(2, 2, *flat),
+            buffer(2, 2, *flat),
+            buffer(2, *flat),
+            buffer(2, *flat),
+            buffer(2, *flat),
+            dma((3,)),
+            dma((2,)), dma((2,)),
+            dma((2, groups)), dma((2, groups)),
+            dma((2,)), dma((2,)),
+            dma((2,)), dma((2,)),
+            dma((2,)), dma((2,)),
+        ],
+        compiler_params=pltpu.CompilerParams(
+            collective_id=0, has_side_effects=True, vmem_limit_bytes=60 * 1024 * 1024
+        ),
+    )(
+        static_control[0], alpha_field[0],
+        perturbations.reshape(variables, levels * rows, cells),
+        static_scale, length_x, length_y, lengths,
+    )
+    return out[None]
+
+
+def fits(mesh):
+    return mesh.shape["sub"] == 8 and mesh.shape["mem"] == 4
+
+
 def solution(mesh):
     return jax.shard_map(
-        body,
+        fused if fits(mesh) else body,
         mesh=mesh,
         in_specs=(
             P("mem", None, "sub", None),

time: 194 us -> 27.6 us (0.14)
  local copies, waits for them, and re-layouts: 61.2 us -> 1.62 us
  matrix products: 41 us -> 0 us
  Pallas kernels: 0 us -> 25.7 us
  waiting for transfers between devices: 23.9 us -> 0 us
  other arithmetic: 21 us -> 0 us
  starting transfers between devices: 16.9 us -> 0 us
  between operations: 14.1 us -> 0.01 us
  blocking collectives: 13.8 us -> 0 us
    dot_general x110 -> x0, matrix products: 41 us -> none  [the longest x52 27.5 us: advance(): jnp.einsum('blrj,lij->blri', current, full_power, precision=lax.Precision...]
    pallas_call x0 -> x1, Pallas kernels: none -> 25.7 us  [fused(): pl.pallas_call(functools.partial(kernel, groups, levels), out_shape=jax.S...]
    all_to_all x3 -> x0, starting transfers between devices: 16.7 us -> none  [the longest x1 7.28 us: body(): lax.all_to_all(member_x, 'sub', split_axis=3, concat_axis=2, tiled=True)]
    unnamed x40 -> x1, local copies, waits for them, and re-layouts: 17.7 us -> 1.62 us
    psum x1 -> x0, waiting for transfers between devices: 15.7 us -> none  [body(): summed = lax.psum(partial_sum, 'mem')]
    all_to_all x1 -> x0, blocking collectives: 13.8 us -> none  [body(): lax.all_to_all(column_filter(lax.all_to_all(member_x, 'sub', split_axis=3...]
    while x144 -> x0, local copies, waits for them, and re-layouts: 10.3 us -> none
    all_to_all x3 -> x0, waiting for transfers between devices: 8.16 us -> none  [the longest x1 8.16 us: body(): lax.all_to_all(column_filter(lax.all_to_all(static_x, 'sub', split_axis=3...]
  transfers between devices with their start and end apart: 4 -> 0, of which waited for: 2 -> 0; matrix products, arithmetic and copies ran while one was open for 31% -> 0% of each run, Pallas kernels for 0% -> 0%
where the time goes in v2:
time: 27.6 us; the launch traced here: 27.3 us
  Pallas kernels  25.7 us (93%)
  local copies, waits for them, and re-layouts  1.62 us (6%)
    pallas_call x1, Pallas kernels, fused(): pl.pallas_call(functools.partial(kernel, groups, levels), out_shape=jax.S...  25.7 us
    unnamed x1, local copies, waits for them, and re-layouts  1.62 us

profile of v2, /device:TPU:0, one launch (start us, length us, event | category | flops | bytes accessed | tf_op | source)
XLA Modules:
  0.0 27.3 jit_solution(11538772080616276228)
XLA Ops:
  0.0 25.7 %shard_map.73 = f32[4,8,1536]{2,1,0:T(8,128)} custom-call(f32[4,8,1536]{2,1,0:T(8,128)} %bitcast.6, f32[4,8,1536]{2,1,0:T(8,128)} %bitcast.7, bf16[4,32,1536]{2,1,0:T(8,128)(2,1)} %bitcast.5, f32[1,4]{1,0:T(1,128)} %scale_ref.1, f32[4]{0:T(128)} %lx_ref.1, f32[4]{0:T(128)} %ly_ref.1, s32[8]{0:T(128)} %len_ref.1), custom_call_target="tpu_custom_call" | custom-call | tf_op jit(solution)/shard_map/pallas_call | solution.py:471
  25.7 1.6 %copy.9 = f32[1,4,8,1536]{3,2,1,0:T(8,128)} copy(f32[1,4,8,1536]{3,2,1,0:T(8,128)} %bitcast.4) | data formatting | bytes 393216

commit v3 on v2

--- a/solution.py
+++ b/solution.py
@@ -126,6 +126,7 @@
 
 
 MESH = pl.DeviceIdType.MESH
+PARTS = 2
 BLK = 128
 HIGHEST = lax.Precision.HIGHEST
 
@@ -286,8 +287,9 @@
     top = mem // 2
     state_rows = 4 * levels
     half_rows = 8 * levels
-    width = static_ref.shape[2] // 2
-    per_half = width // BLK
+    width = static_ref.shape[2] // (2 * PARTS)
+    per_part = width // BLK
+    units = 2 * PARTS
 
     loads = [
         pltpu.make_async_copy(src, dst, load.at[which])
@@ -356,17 +358,17 @@
             device_id=(beside, mem), device_id_type=MESH,
         )
 
-    def to_near(half):
-        return pltpu.make_async_remote_copy(
-            src_ref=part.at[half], dst_ref=fold.at[half],
-            send_sem=send4.at[half], recv_sem=recv4.at[half],
+    def to_near(half, piece):
+        return pltpu.make_async_remote_copy(
+            src_ref=part.at[half, piece], dst_ref=fold.at[half, piece],
+            send_sem=send4.at[half, piece], recv_sem=recv4.at[half, piece],
             device_id=(me, near), device_id_type=MESH,
         )
 
-    def to_far(half):
-        return pltpu.make_async_remote_copy(
-            src_ref=give.at[half], dst_ref=take.at[half],
-            send_sem=send5.at[half], recv_sem=recv5.at[half],
+    def to_far(half, piece):
+        return pltpu.make_async_remote_copy(
+            src_ref=give.at[half, piece], dst_ref=take.at[half, piece],
+            send_sem=send5.at[half, piece], recv_sem=recv5.at[half, piece],
             device_id=(me, far), device_id_type=MESH,
         )
 
@@ -375,13 +377,17 @@
         for level in range(levels):
             cells = smooth_x(jnp.where(valid, ref[level], 0.0), ahead[level], back[level])
             for half in range(2):
-                outgo[field, half, 8 * level : 8 * level + 8] = jnp.concatenate(
-                    cells[half * per_half : (half + 1) * per_half], axis=1
-                )
+                for piece in range(PARTS):
+                    first = (half * PARTS + piece) * per_part
+                    outgo[field * PARTS + piece, half, 8 * level : 8 * level + 8] = jnp.concatenate(
+                        cells[first : first + per_part], axis=1
+                    )
         if field == 0:
             pl.semaphore_wait(barrier, len(friends))
-        to_pair(field).start()
-        pair[field, side] = outgo[field, side]
+        for unit in range(field * PARTS, (field + 1) * PARTS):
+            to_pair(unit).start()
+        for unit in range(field * PARTS, (field + 1) * PARTS):
+            pair[unit, side] = outgo[unit, side]
 
     moments, inner, outer = line_matrices(group, groups, levels, lx_ref, ly_ref, len_ref)
     moments, inner, outer = split(moments), split(inner), split(outer)
@@ -389,13 +395,16 @@
     def pair_rows(field):
         return jnp.concatenate([pair[field, 0], pair[field, 1]], axis=0)
 
-    for field in range(2):
+    def spread(field):
         from_pair(field).wait_recv()
         both = product(moments, pair_rows(field))
         for kind in range(2):
             mom[field, kind] = both[kind * state_rows : (kind + 1) * state_rows]
         for step in range(1, groups):
             to_group(field, step).start()
+
+    for piece in range(PARTS):
+        spread(piece)
 
     def finish(field):
         mixed = product(inner, pair_rows(field))
@@ -408,58 +417,72 @@
         to_home(field).start()
         done[field, side] = jnp.where(side == 0, mine, theirs)
 
-    def terms(half, variable):
-        columns = pl.ds(pl.multiple_of(half * width, BLK), width)
-        return pert_ref[variable, :, columns].astype(jnp.float32) * done[0, half]
-
-    def gather(half):
+    def columns(half, piece):
+        return pl.ds(pl.multiple_of((half * PARTS + piece) * width, BLK), width)
+
+    def terms(half, piece, variable):
+        return pert_ref[variable, :, columns(half, piece)].astype(jnp.float32) * done[piece, half]
+
+    def gather(half, piece):
         for which in range(2):
-            part[half, which] = terms(half, 2 * which + 1 - core)
-        to_near(half).start()
-
-    def forward_sum(half):
-        to_near(half).wait_recv()
-        give[half] = terms(half, 2 * (1 - top) + core) + fold[half, 1 - top]
-        to_far(half).start()
-        own[half] = terms(half, 2 * top + core) + fold[half, top]
-
-    finish(0)
-    loads[2].wait()
-    gather(side)
-    forward_sum(side)
-    from_home(0).wait_recv()
-    gather(1 - side)
-    forward_sum(1 - side)
-    finish(1)
-
-    def write(half):
-        to_far(half).wait_recv()
-        total = (own[half] + take[half]) * 0.5
-        columns = pl.ds(pl.multiple_of(half * width, BLK), width)
+            part[half, piece, which] = terms(half, piece, 2 * which + 1 - core)
+        to_near(half, piece).start()
+
+    def forward_sum(half, piece):
+        to_near(half, piece).wait_recv()
+        give[half, piece] = (
+            terms(half, piece, 2 * (1 - top) + core) + fold[half, piece, 1 - top]
+        )
+        to_far(half, piece).start()
+        own[half, piece] = terms(half, piece, 2 * top + core) + fold[half, piece, top]
+
+    def write(half, piece):
+        to_far(half, piece).wait_recv()
+        total = (own[half, piece] + take[half, piece]) * 0.5
         for level in range(levels):
             rows = slice(8 * level, 8 * level + 8)
-            out_ref[level, :, columns] = (
-                scale_ref[0, level] * done[1, half, rows] + total[rows]
+            out_ref[level, :, columns(half, piece)] = (
+                scale_ref[0, level] * done[PARTS + piece, half, rows] + total[rows]
             )
 
-    write(side)
-    from_home(1).wait_recv()
-    write(1 - side)
-    for field in range(2):
+    pieces = range(PARTS)
+    for piece in pieces:
+        finish(piece)
+        if piece == 0:
+            loads[2].wait()
+        gather(side, piece)
+        spread(PARTS + piece)
+    for piece in pieces:
+        forward_sum(side, piece)
+        from_home(piece).wait_recv()
+        gather(1 - side, piece)
+    finish(PARTS)
+    for piece in pieces:
+        forward_sum(1 - side, piece)
+    for piece in range(1, PARTS):
+        finish(PARTS + piece)
+    for piece in pieces:
+        write(side, piece)
+    for piece in pieces:
+        from_home(PARTS + piece).wait_recv()
+        write(1 - side, piece)
+    for field in range(units):
         to_pair(field).wait_send()
         to_home(field).wait_send()
         for step in range(1, groups):
             to_group(field, step).wait_send()
     for half in (side, 1 - side):
-        to_near(half).wait_send()
-        to_far(half).wait_send()
+        for piece in pieces:
+            to_near(half, piece).wait_send()
+            to_far(half, piece).wait_send()
 
 
 def fused(static_control, alpha_field, perturbations, static_scale, length_x, length_y, lengths):
     groups = lax.axis_size("sub") // 2
     unused, levels, rows, cells = static_control.shape
     variables = perturbations.shape[1]
-    width = cells // 2
+    width = cells // (2 * PARTS)
+    units = 2 * PARTS
     flat = (levels * rows, width)
     anywhere = pl.BlockSpec(memory_space=pl.ANY)
     smem = pl.BlockSpec(memory_space=pltpu.SMEM)
@@ -479,23 +502,23 @@
             pltpu.VMEM((variables, levels * rows, cells), jnp.bfloat16),
             pltpu.VMEM((levels, 2 * BLK, 2 * BLK), jnp.bfloat16),
             pltpu.VMEM((levels, 2 * BLK, 2 * BLK), jnp.bfloat16),
-            buffer(2, 2, *flat),
-            buffer(2, 2, *flat),
-            buffer(2, 2, 4 * levels, width),
-            buffer(2, groups - 1, 4 * levels, width),
-            buffer(2, *flat),
-            buffer(2, 2, *flat),
-            buffer(2, 2, *flat),
-            buffer(2, 2, *flat),
-            buffer(2, *flat),
-            buffer(2, *flat),
-            buffer(2, *flat),
+            buffer(units, 2, *flat),
+            buffer(units, 2, *flat),
+            buffer(units, 2, 4 * levels, width),
+            buffer(units, groups - 1, 4 * levels, width),
+            buffer(units, *flat),
+            buffer(units, 2, *flat),
+            buffer(2, PARTS, 2, *flat),
+            buffer(2, PARTS, 2, *flat),
+            buffer(2, PARTS, *flat),
+            buffer(2, PARTS, *flat),
+            buffer(2, PARTS, *flat),
             dma((3,)),
-            dma((2,)), dma((2,)),
-            dma((2, groups)), dma((2, groups)),
-            dma((2,)), dma((2,)),
-            dma((2,)), dma((2,)),
-            dma((2,)), dma((2,)),
+            dma((units,)), dma((units,)),
+            dma((units, groups)), dma((units, groups)),
+            dma((units,)), dma((units,)),
+            dma((2, PARTS)), dma((2, PARTS)),
+            dma((2, PARTS)), dma((2, PARTS)),
         ],
         compiler_params=pltpu.CompilerParams(
             collective_id=0, has_side_effects=True, vmem_limit_bytes=60 * 1024 * 1024

time: 27.6 us -> 26.7 us (0.967)
  Pallas kernels: 25.7 us -> 24.9 us
    pallas_call x1, Pallas kernels: 25.7 us -> 24.9 us  [fused(): pl.pallas_call(functools.partial(kernel, groups, levels), out_shape=jax.S...]
where the time goes in v3:
time: 26.7 us; the launch traced here: 26.5 us
  Pallas kernels  24.9 us (93%)
  local copies, waits for them, and re-layouts  1.62 us (6%)
    pallas_call x1, Pallas kernels, fused(): pl.pallas_call(functools.partial(kernel, groups, levels), out_shape=jax.S...  24.9 us
    unnamed x1, local copies, waits for them, and re-layouts  1.62 us

profile of v3, /device:TPU:0, one launch (start us, length us, event | category | flops | bytes accessed | tf_op | source)
XLA Modules:
  0.0 26.5 jit_solution(16319043734915004957)
XLA Ops:
  0.0 24.9 %shard_map.73 = f32[4,8,1536]{2,1,0:T(8,128)} custom-call(f32[4,8,1536]{2,1,0:T(8,128)} %bitcast.6, f32[4,8,1536]{2,1,0:T(8,128)} %bitcast.7, bf16[4,32,1536]{2,1,0:T(8,128)(2,1)} %bitcast.5, f32[1,4]{1,0:T(1,128)} %scale_ref.1, f32[4]{0:T(128)} %lx_ref.1, f32[4]{0:T(128)} %ly_ref.1, s32[8]{0:T(128)} %len_ref.1), custom_call_target="tpu_custom_call" | custom-call | tf_op jit(solution)/shard_map/pallas_call | solution.py:494
  24.9 1.6 %copy.9 = f32[1,4,8,1536]{3,2,1,0:T(8,128)} copy(f32[1,4,8,1536]{3,2,1,0:T(8,128)} %bitcast.4) | data formatting | bytes 393216
